TPU v7x, 32 devices: a whole 2x2x4 slice. The times are simulated.
32 devices in a mesh: grp: 2 (over x), exp: 8 (over z, y), tp: 2 (over core).
Axes of the slice: x: 2, y: 2, z: 4, core: 2. Of those that a mesh axis runs over, the one named last changes fastest.
Arguments:
- tokens: bfloat16 [4096, 2304], P(('grp', 'exp', 'tp')), parts along dimension 0, may hold values from -12 to 12
- router: bfloat16 [2304, 8], replicated, may hold values from -0.03125 to 0.03125
- expert_ids: int32 [4096, 4], P(('grp', 'exp', 'tp')), parts along dimension 0, may hold values from 0 to 7, all different within a row; in each aligned block of 128 rows (0 to 127, 128 to 255, ...) at most 80 rows name the same one
- gate_weight: bfloat16 [8, 2304, 1536], P('exp', None, 'tp'), may hold values from -0.125 to 0.125
- up_weight: bfloat16 [8, 2304, 1536], P('exp', None, 'tp'), may hold values from -0.125 to 0.125
- down_weight: bfloat16 [8, 1536, 2304], P('exp', 'tp'), may hold values from -0.15625 to 0.15625
Outputs:
- combined: bfloat16 [4096, 2304], P(('grp', 'exp', 'tp')), parts along dimension 0
There are 2 independent parts, one for each index of `grp`. A program takes and returns all parts, laid end to end along the dimension named above; an argument that names none is the same for every part. Nothing has to cross between parts.
Inputs may be any that keep to these rules, and one draw needn't show every extreme that they name: `expert_ids`: each row names 4 different experts; among the 128 rows of one device no expert is named more than 80 times, a bound that some block reaches.
All inputs are finite; a program needn't handle non-finite values.
Results may differ from a plain program's by a relative error of at most 0.0068.
Values may be sent and summed in bfloat16 or wider, within the bound.
A program may use at most 128 MiB of HBM per device.

v0:
```python
import jax
import jax.numpy as jnp
from jax import lax
from jax.sharding import PartitionSpec as P


def slot_numbers(choices_flat, expert_count):
    onehot = (choices_flat[:, None] == jnp.arange(expert_count, dtype=jnp.int32)[None, :]).astype(
        jnp.int32
    )
    before = jnp.cumsum(onehot, axis=0) - onehot
    return jnp.sum(before * onehot, axis=1)


def router_gates(tokens, router, expert_ids):
    logits = jnp.dot(tokens, router, preferred_element_type=jnp.float32)
    chosen = jnp.take_along_axis(logits, expert_ids, axis=1)
    raised = jnp.exp(chosen)
    return raised / jnp.sum(raised, axis=1, keepdims=True)


def swiglu_part(slot_rows, gate_part, up_part, down_part):
    gate_act = jnp.dot(slot_rows, gate_part, preferred_element_type=jnp.float32)
    lifted = jnp.dot(slot_rows, up_part, preferred_element_type=jnp.float32)
    gate_act = jnp.minimum(gate_act, 7.0)
    lifted = jnp.clip(lifted, -7.0, 7.0)
    hidden = ((lifted + 1.0) * gate_act * jax.nn.sigmoid(1.702 * gate_act)).astype(jnp.bfloat16)
    return jnp.dot(hidden, down_part, preferred_element_type=jnp.float32).astype(jnp.bfloat16)


def on_device(tokens, router, expert_ids, gate_weight, up_weight, down_weight):
    tok_rows, model_width = tokens.shape
    top_count = expert_ids.shape[1]
    experts_all = router.shape[1]
    capacity = min(
        tok_rows, max(2, (5 * tok_rows * top_count + 4 * experts_all - 1) // (4 * experts_all))
    )
    gate_share = router_gates(tokens, router, expert_ids)
    flat_ids = expert_ids.reshape(-1)
    target = flat_ids * capacity + slot_numbers(flat_ids, experts_all)
    slot_ids = jnp.arange(experts_all * capacity, dtype=jnp.int32)
    placing = (slot_ids[:, None] == target[None, :]).astype(jnp.bfloat16)
    placing = placing.reshape(experts_all * capacity, tok_rows, top_count).sum(axis=2)
    outgoing = jnp.dot(placing, tokens, preferred_element_type=jnp.float32).astype(jnp.bfloat16)
    outgoing = outgoing.reshape(experts_all, capacity, model_width)
    gate_local = gate_weight[0]
    up_local = up_weight[0]
    down_local = down_weight[0]
    tp_count = lax.axis_size("tp")
    received = lax.all_to_all(outgoing, "exp", split_axis=0, concat_axis=0, tiled=True)
    gathered = lax.all_gather(received, "tp", axis=0, tiled=True)
    sources = gathered.shape[0]
    slot_count = gathered.shape[1]
    flattened = gathered.reshape(sources * slot_count, model_width)
    partial_value = swiglu_part(flattened, gate_local, up_local, down_local).reshape(
        sources, slot_count, model_width
    )
    swapped = lax.all_to_all(partial_value, "tp", split_axis=0, concat_axis=0, tiled=True)
    own_count = received.shape[0]
    slot_count = received.shape[1]
    paired = swapped.reshape(tp_count, own_count, slot_count, model_width).astype(jnp.float32)
    own_share = jnp.sum(paired, axis=0).astype(jnp.bfloat16)
    results = lax.all_to_all(own_share, "exp", split_axis=0, concat_axis=0, tiled=True)
    flat_results = results.reshape(experts_all * capacity, model_width)
    picked = flat_results[target].reshape(tok_rows, top_count, model_width).astype(jnp.float32)
    combined = jnp.sum(gate_share[:, :, None] * picked, axis=1)
    return combined.astype(jnp.bfloat16)


def solution(mesh):
    placed = (
        P(("grp", "exp", "tp"), None),
        P(),
        P(("grp", "exp", "tp"), None),
        P("exp", None, "tp"),
        P("exp", None, "tp"),
        P("exp", "tp", None),
    )
    return jax.shard_map(
        on_device,
        mesh=mesh,
        in_specs=placed,
        out_specs=P(("grp", "exp", "tp"), None),
        check_vma=False,
    )
```

profile of v0, /device:TPU:0, one launch (start us, length us, event | category | flops | bytes accessed | tf_op | source)
XLA Modules:
  0.0 260.5 jit_solution(18052666575447784935)
XLA Ops:
  6.5 0.0 copy-start
  6.5 0.0 all-gather.2.cloned.1.call-start
  6.5 1.6 copy.37
  8.1 0.9 eq.44
  9.0 1.5 eq.40
  10.6 0.6 fusion.7
  11.2 2.2 reduce-window.6
  13.4 0.8 slice_reduce_fusion
  14.2 1.3 reduce-window.9
  15.4 0.7 slice.7
  16.1 1.3 fusion.6
  17.4 1.4 reduce_sum.57
  18.8 1.5 broadcast_multiply_fusion
  20.3 0.9 copy.40
  21.2 0.2 fusion.4
  21.3 2.0 convolution_convert_fusion.1
  23.3 74.3 %all_to_all.15 = bf16[8,80,2304]{2,1,0:T(8,128)(2,1)} all-to-all(bf16[8,80,2304]{2,1,0:T(8,128)(2,1)S(1)} %bitcast.44), channel_id=1, replica_groups=mesh['grp'=2,'exp'=8,'tp'=2] {'exp'}, dimensions={0} | all-to-all | bytes 5898240 | tf_op jit(solution)/shard_map/all_to_all | solution.py:50
  97.6 0.0 all-gather.2.cloned.1.call-update
  97.7 14.7 %all-gather.2.cloned.1.call-done = bf16[16,80,2304]{2,1,0:T(8,128)(2,1)} async-done(((bf16[8,80,2304]{2,1,0:T(8,128)(2,1)}), bf16[16,80,2304]{2,1,0:T(8,128)(2,1)}) %all-gather.2.cloned.1.call-update) | async-done | bytes 5898256 | tf_op jit(solution)/shard_map/all_gather | solution.py:51
  112.4 10.4 %convolution_clamp_fusion = f32[1280,768]{1,0:T(8,128)} fusion(bf16[1280,2304]{1,0:T(8,128)(2,1)} %bitcast.48, bf16[1,2304,768]{2,1,0:T(8,128)(2,1)} %param.10), kind=kOutput, calls=%fused_computation.5 | convolution fusion | flops 4530831360 | bytes 13369344 | tf_op jit(solution)/shard_map/dot_general | solution.py:24
  122.8 0.0 copy-done
  122.8 17.4 %convolution_convert_fusion = bf16[1280,2304]{1,0:T(8,128)(2,1)} fusion(bf16[1,768,2304]{2,1,0:T(8,128)(2,1)S(1)} %copy-done, bf16[1280,2304]{1,0:T(8,128)(2,1)} %bitcast.49, f32[1280,768]{1,0:T(8,128)} %convolution_clamp_fusion, bf16[1,2304,768]{2,1,0:T(8,128)(2,1)} %param.9), kind=kOutput, calls=%fused_computation.2 | convolution fusion | flops 9071493120 | bytes 22806528 | tf_op jit(solution)/shard_map/dot_general | solution.py:28
  140.2 14.7 %all_to_all.16 = bf16[16,80,2304]{2,1,0:T(8,128)(2,1)} all-to-all(bf16[16,80,2304]{2,1,0:T(8,128)(2,1)} %bitcast.45), channel_id=1, replica_groups=mesh['grp'=2,'exp'=8,'tp'=2] {'tp'}, dimensions={0} | all-to-all | bytes 11796480 | tf_op jit(solution)/shard_map/all_to_all | solution.py:58
  154.9 6.2 %reduce_sum.59 = bf16[8,80,2304]{2,1,0:T(8,128)(2,1)} reduce(bf16[2,8,80,2304]{3,2,1,0:T(8,128)(2,1)} %bitcast.43, bf16[]{:T(256)} %constant.35.clone.1), dimensions={0}, to_apply=%region_5.6 | reduce | flops 1474560 | bytes 8847362 | tf_op jit(solution)/shard_map/reduce_sum | solution.py:62
  161.1 0.0 copy-start.1
  161.1 5.9 %all-to-all-start.2 = ((bf16[8,80,2304]{2,1,0:T(8,128)(2,1)}), bf16[8,80,2304]{2,1,0:T(8,128)(2,1)}, u32[]{:S(2)}, u32[]{:S(2)}) async-start(bf16[8,80,2304]{2,1,0:T(8,128)(2,1)} %reduce_sum.59), calls=%async_computation.2 | async-start | bytes 5898240 | tf_op jit(solution)/shard_map/all_to_all | solution.py:63
  167.0 1.5 mul.51
  168.5 0.0 copy-done.1
  168.5 0.7 copy.34
  169.2 0.9 reshape.118
  170.2 1.3 fusion.10
  171.5 2.6 gather_fusion.1
  174.1 0.7 reshape.121
  174.8 0.9 copy.35
  175.8 0.7 copy.36
  176.5 0.6 compare_select_fusion
  177.2 56.7 %all-to-all-done.2 = bf16[8,80,2304]{2,1,0:T(8,128)(2,1)} async-done(((bf16[8,80,2304]{2,1,0:T(8,128)(2,1)}), bf16[8,80,2304]{2,1,0:T(8,128)(2,1)}, u32[]{:S(2)}, u32[]{:S(2)}) %all-to-all-start.2) | async-done | bytes 2949152 | tf_op jit(solution)/shard_map/all_to_all | solution.py:63
  233.9 8.0 %gather_fusion = bf16[512,2304]{1,0:T(8,128)(2,1)} fusion(bf16[640,2304]{1,0:T(8,128)(2,1)} %bitcast.10, s32[1024]{0:T(1024)S(1)} %pad_clamp_fusion), kind=kCustom, calls=%fused_computation | custom fusion | bytes 4720640 | tf_op jit(solution)/shard_map/gather | solution.py:65
  241.9 5.3 %reshape.109 = f32[128,4,2304]{2,1,0:T(4,128)} reshape(bf16[512,2304]{1,0:T(8,128)(2,1)} %gather_fusion) | data formatting | bytes 7077888 | tf_op jit(solution)/shard_map/convert_element_type | solution.py:65
  247.1 6.5 %multiply_reduce_fusion = bf16[128,2304]{1,0:T(8,128)(2,1)} fusion(f32[128,4,2304]{2,1,0:T(4,128)} %reshape.109, f32[128,4]{1,0:T(8,128)} %copy.36), kind=kLoop, calls=%fused_computation.4 | loop fusion | flops 2064384 | bytes 5310464 | tf_op jit(solution)/shard_map/reduce_sum | solution.py:66
  (4 shorter events, 0.1 us)
Async XLA Ops:
  6.5 116.3 %copy-start = (bf16[1,768,2304]{2,1,0:T(8,128)(2,1)S(1)}, bf16[1,768,2304]{2,1,0:T(8,128)(2,1)}, u32[]{:S(2)}) copy-start(bf16[1,768,2304]{2,1,0:T(8,128)(2,1)} %param.11) | copy-start | bytes 10616836
  6.5 105.8 %all-gather.2.cloned.1.call-start = ((), (), s32[]{:S(2)}) async-start(), calls=%async_computation.3 | async-start | bytes 8847360 | tf_op jit(solution)/shard_map/all_gather | solution.py:51
  161.1 7.4 %copy-start.1 = (s32[128,4]{0,1:T(4,128)S(1)}, s32[128,4]{0,1:T(4,128)}, u32[]{:S(2)}) copy-start(s32[128,4]{0,1:T(4,128)} %param.8) | copy-start | bytes 6148
  161.1 72.8 %all-to-all-start.2 = ((bf16[8,80,2304]{2,1,0:T(8,128)(2,1)}), bf16[8,80,2304]{2,1,0:T(8,128)(2,1)}, u32[]{:S(2)}, u32[]{:S(2)}) async-start(bf16[8,80,2304]{2,1,0:T(8,128)(2,1)} %reduce_sum.59), calls=%async_computation.2 | async-start | bytes 5898240 | tf_op jit(solution)/shard_map/all_to_all | solution.py:63
Sparse Core Ops, SparseCore 0:
  97.8 14.5 all-gather.1
where the time goes:
time: 262 us; the launch traced here: 261 us
  blocking collectives  89 us (34%)
  waiting for transfers between devices  71.5 us (27%)
  matrix products  31.1 us (12%)
  local copies, waits for them, and re-layouts  29.1 us (11%)
  other arithmetic  20.5 us (8%)
  between operations  13.4 us (5%)
  starting transfers between devices  5.91 us (2%)
    all_to_all x1, blocking collectives, on_device(): lax.all_to_all(outgoing, 'exp', split_axis=0, concat_axis=0, tiled=True)  74.3 us
    all_to_all x1, waiting for transfers between devices, on_device(): lax.all_to_all(own_share, 'exp', split_axis=0, concat_axis=0, tiled=True)  56.7 us
    dot_general x1, matrix products, swiglu_part(): jnp.dot(hidden, down_part, preferred_element_type=jnp.float32)  17.4 us
    all_gather x1, waiting for transfers between devices, on_device(): gathered = lax.all_gather(received, 'tp', axis=0, tiled=True)  14.7 us
    all_to_all x1, blocking collectives, on_device(): lax.all_to_all(partial_value, 'tp', split_axis=0, concat_axis=0, tiled=True)  14.7 us
    dot_general x1, matrix products, swiglu_part(): lifted = jnp.dot(slot_rows, up_part, preferred_element_type=jnp.float32)  10.4 us
    gather x1, local copies, waits for them, and re-layouts, on_device(): flat_results[target].reshape(tok_rows, top_count, model_width)  7.96 us
    reduce_sum x1, other arithmetic, on_device(): combined = jnp.sum(gate_share[:, :, None] * picked, axis=1)  6.54 us
  transfers between devices with their start and end apart: 2, of which 2 were waited for; matrix products, arithmetic and copies ran while one was open for 4% of the time, Pallas kernels for 0%

commit v1 on v0

--- a/solution.py
+++ b/solution.py
@@ -1,7 +1,389 @@
+import functools
+
 import jax
 import jax.numpy as jnp
 from jax import lax
+from jax.experimental import pallas as pl
+from jax.experimental.pallas import tpu as pltpu
 from jax.sharding import PartitionSpec as P
+
+MESH = pl.DeviceIdType.MESH
+STEPS = 4
+F32 = jnp.float32
+BF16 = jnp.bfloat16
+
+
+def moe_kernel(
+    cap,
+    chunks,
+    tok_ref,
+    router_ref,
+    ids_ref,
+    wg_hbm,
+    wu_hbm,
+    wd_hbm,
+    out_ref,
+    wg,
+    wu,
+    wd,
+    tok,
+    gates,
+    slots,
+    ypack,
+    own,
+    tpout,
+    tpin,
+    yret,
+    comb,
+    acc,
+    rout,
+    inbox,
+    w_sem,
+    tok_s,
+    tok_r,
+    gate_s,
+    gate_r,
+    ys_s,
+    ys_r,
+    t0_s,
+    t0_r,
+    t2_s,
+    t2_r,
+    tp_s,
+    tp_r,
+    yr_s,
+    yr_r,
+    rs_s,
+    rs_r,
+):
+    rows, width = tok_ref.shape
+    experts = router_ref.shape[1]
+    top = ids_ref.shape[1]
+    grp, exp, tp = lax.axis_index("grp"), lax.axis_index("exp"), lax.axis_index("tp")
+    z, y = exp // 2, exp % 2
+    adj_z = z + 1 - 2 * (z % 2)
+    across_z = 3 - z
+    other_exp = exp + 1 - 2 * y
+    adj = (grp, adj_z * 2 + y, tp)
+    across = (grp, across_z * 2 + y, tp)
+    ynb = (grp, other_exp, tp)
+    tpn = (grp, exp, 1 - tp)
+    middle = jnp.logical_or(z == 1, z == 2)
+    edge = jnp.logical_or(z == 0, z == 3)
+
+    loads = [
+        pltpu.make_async_copy(src.at[0], dst, w_sem.at[n])
+        for n, (src, dst) in enumerate(((wg_hbm, wg), (wu_hbm, wu), (wd_hbm, wd)))
+    ]
+    for load in loads:
+        load.start()
+
+    barrier = pltpu.get_barrier_semaphore()
+    for peer in (adj, ynb, tpn):
+        pl.semaphore_signal(barrier, inc=1, device_id=peer, device_id_type=MESH)
+
+    @pl.when(middle)
+    def _():
+        pl.semaphore_signal(barrier, inc=1, device_id=across, device_id_type=MESH)
+        pl.semaphore_wait(barrier, 4)
+
+    @pl.when(edge)
+    def _():
+        pl.semaphore_wait(barrier, 3)
+
+    def remote(src, dst, send, recv, peer):
+        return pltpu.make_async_remote_copy(
+            src_ref=src,
+            dst_ref=dst,
+            send_sem=send,
+            recv_sem=recv,
+            device_id=peer,
+            device_id_type=MESH,
+        )
+
+    def tok_copy(n, source, target, peer):
+        src = tok_ref if source == 0 else tok.at[source - 1]
+        return remote(src, tok.at[target - 1], tok_s.at[n], tok_r.at[target - 1], peer)
+
+    def gate_copy(n, source, target, peer):
+        return remote(gates.at[source], gates.at[target], gate_s.at[n], gate_r.at[target - 1], peer)
+
+    hops = ((0, 0, 1, adj), (1, 0, 2, across), (2, 1, 3, across), (3, 2, 2, adj), (4, 3, 3, adj))
+
+    tok_copy(*hops[0]).start()
+
+    @pl.when(middle)
+    def _():
+        tok_copy(*hops[1]).start()
+
+    logits = jnp.dot(tok_ref[...], router_ref[...], preferred_element_type=F32)
+    lane = lax.broadcasted_iota(jnp.int32, (rows, experts), 1)
+    ids = ids_ref[...]
+    chosen = jnp.zeros((rows, experts), F32)
+    for k in range(top):
+        chosen = jnp.where(lane == ids[:, k : k + 1], 1.0, chosen)
+    raised = jnp.where(chosen > 0.0, jnp.exp(logits), 0.0)
+    share = raised / jnp.sum(raised, axis=1, keepdims=True)
+    wide = jnp.concatenate([share, jnp.zeros((rows, 128 - experts), F32)], axis=1)
+    gates[0] = wide.T[:experts]
+    gate_copy(*hops[0]).start()
+
+    @pl.when(middle)
+    def _():
+        gate_copy(*hops[1]).start()
+
+    def placing(i, weighted):
+        g8 = gates[i]
+        m8 = jnp.where(g8 > 0.0, 1.0, 0.0)
+        before = lax.broadcasted_iota(jnp.int32, (rows, rows), 0)
+        after = lax.broadcasted_iota(jnp.int32, (rows, rows), 1)
+        earlier = jnp.where(before < after, 1.0, 0.0).astype(BF16)
+        pos8 = jnp.dot(m8.astype(BF16), earlier, preferred_element_type=F32)
+        pos8 = jnp.where(m8 > 0.0, pos8, -1000.0)
+        which = lax.broadcasted_iota(jnp.int32, (experts, rows), 0)
+
+        def pick(table, number):
+            return jnp.sum(jnp.where(which == number, table, 0.0), axis=0, keepdims=True)
+
+        slot = lax.broadcasted_iota(jnp.int32, (2 * cap, rows), 0)
+        mine = slot < cap
+        wanted = jnp.where(mine, pick(pos8, exp), pick(pos8, other_exp) + float(cap))
+        value = jnp.where(mine, pick(g8, exp), pick(g8, other_exp)) if weighted else 1.0
+        return jnp.where(wanted == slot.astype(F32), value, 0.0)
+
+    def ysend(i):
+        return remote(ypack.at[i], slots.at[i, pl.ds(cap, cap)], ys_s.at[i], ys_r.at[i], ynb)
+
+    def tsend0(i):
+        return remote(
+            slots.at[i, pl.ds(0, cap)], slots.at[i, pl.ds(2 * cap, cap)], t0_s.at[i], t0_r.at[i], tpn
+        )
+
+    def tsend2(i):
+        return remote(
+            slots.at[i, pl.ds(cap, cap)], slots.at[i, pl.ds(3 * cap, cap)], t2_s.at[i], t2_r.at[i], tpn
+        )
+
+    def psend(i):
+        return remote(tpout.at[i], tpin.at[i], tp_s.at[i], tp_r.at[i], tpn)
+
+    def yback(i):
+        return remote(yret.at[i], comb.at[i, pl.ds(cap, cap)], yr_s.at[i], yr_r.at[i], ynb)
+
+    def step_pack(i):
+        place = placing(i, False).astype(BF16)
+        block = tok_ref if i == 0 else tok.at[i - 1]
+        ypack[i] = jnp.dot(place[cap:], block[...], preferred_element_type=F32).astype(BF16)
+        ysend(i).start()
+        slots[i, pl.ds(0, cap)] = jnp.dot(
+            place[:cap], block[...], preferred_element_type=F32
+        ).astype(BF16)
+        tsend0(i).start()
+
+    def step_share(i):
+        ysend(i).wait_recv()
+        tsend2(i).start()
+
+    def step_experts(i):
+        tsend0(i).wait_recv()
+        tsend2(i).wait_recv()
+        block = slots[i]
+        gate_act = jnp.minimum(jnp.dot(block, wg[...], preferred_element_type=F32), 7.0)
+        lifted = jnp.clip(jnp.dot(block, wu[...], preferred_element_type=F32), -7.0, 7.0)
+        hidden = ((lifted + 1.0) * gate_act * jax.nn.sigmoid(1.702 * gate_act)).astype(BF16)
+        part = width // 3
+        for c in range(3):
+            at = pl.ds(c * part, part)
+            result = jnp.dot(hidden, wd[:, at], preferred_element_type=F32)
+            own[:, at] = result[: 2 * cap]
+            tpout[i, :, at] = result[2 * cap :].astype(BF16)
+        psend(i).start()
+
+    def step_join(i):
+        psend(i).wait_recv()
+        yret[i] = (own[cap:] + tpin[i, pl.ds(cap, cap)].astype(F32)).astype(BF16)
+        yback(i).start()
+        comb[i, pl.ds(0, cap)] = (own[:cap] + tpin[i, pl.ds(0, cap)].astype(F32)).astype(BF16)
+
+    def step_combine(i):
+        yback(i).wait_recv()
+        weight = placing(i, True)
+        high = weight.astype(BF16)
+        low = (weight - high.astype(F32)).astype(BF16)
+        block = comb[i]
+        turned = (((0,), (0,)), ((), ()))
+        acc[i] = lax.dot_general(high, block, turned, preferred_element_type=F32) + lax.dot_general(
+            low, block, turned, preferred_element_type=F32
+        )
+
+    def arrive(phase):
+        def take(step):
+            tok_copy(0, 0, step, adj).wait_recv()
+            gate_copy(0, 0, step, adj).wait_recv()
+
+        def give(n):
+            tok_copy(*hops[n]).start()
+            gate_copy(*hops[n]).start()
+
+        @pl.when(edge)
+        def _():
+            take(phase)
+
+        @pl.when(middle)
+        def _():
+            if phase == 1:
+                take(1)
+                give(2)
+                take(2)
+                give(3)
+            elif phase == 2:
+                take(3)
+                give(4)
+
+    span = width // chunks
+
+    def sum_copy(i, slot, c, peer):
+        at = pl.ds(c * span, span)
+        return remote(
+            rout.at[i - 1, :, at],
+            inbox.at[slot, :, at],
+            rs_s.at[(i - 1) * chunks + c],
+            rs_r.at[slot * chunks + c],
+            peer,
+        )
+
+    def edge_send(i):
+        @pl.when(edge)
+        def _():
+            for c in range(chunks):
+                at = pl.ds(c * span, span)
+                rout[i - 1, :, at] = acc[i, :, at].astype(BF16)
+                sum_copy(i, i - 1, c, adj).start()
+
+    def middle_send(i, arrived, slot, peer):
+        for c in range(chunks):
+            at = pl.ds(c * span, span)
+            sum_copy(1, arrived, c, adj).wait_recv()
+            rout[i - 1, :, at] = (acc[i, :, at] + inbox[arrived, :, at].astype(F32)).astype(BF16)
+            sum_copy(i, slot, c, peer).start()
+
+    step_pack(0)
+    step_share(0)
+    arrive(1)
+    step_pack(1)
+    for load in loads:
+        load.wait()
+    step_experts(0)
+    step_join(0)
+    step_share(1)
+    arrive(2)
+    step_pack(2)
+    step_combine(0)
+    step_experts(1)
+    step_join(1)
+    step_share(2)
+    arrive(3)
+    step_pack(3)
+    step_combine(1)
+    edge_send(1)
+    step_experts(2)
+    step_join(2)
+    step_share(3)
+    step_experts(3)
+    step_join(3)
+    step_combine(2)
+    edge_send(2)
+    step_combine(3)
+    edge_send(3)
+
+    @pl.when(middle)
+    def _():
+        middle_send(2, 1, 3, across)
+        middle_send(3, 2, 4, across)
+        middle_send(1, 4, 0, adj)
+        for c in range(chunks):
+            at = pl.ds(c * span, span)
+            sum_copy(1, 0, c, adj).wait_recv()
+            sum_copy(1, 3, c, adj).wait_recv()
+            out_ref[:, at] = (
+                acc[0, :, at] + inbox[0, :, at].astype(F32) + inbox[3, :, at].astype(F32)
+            ).astype(BF16)
+
+    @pl.when(edge)
+    def _():
+        for c in range(chunks):
+            at = pl.ds(c * span, span)
+            sum_copy(1, 0, c, adj).wait_recv()
+            out_ref[:, at] = (acc[0, :, at] + inbox[0, :, at].astype(F32)).astype(BF16)
+
+    tok_copy(*hops[0]).wait_send()
+    gate_copy(*hops[0]).wait_send()
+
+    @pl.when(middle)
+    def _():
+        for n in range(1, 5):
+            tok_copy(*hops[n]).wait_send()
+            gate_copy(*hops[n]).wait_send()
+
+    for i in range(STEPS):
+        for copy in (ysend(i), tsend0(i), tsend2(i), psend(i), yback(i)):
+            copy.wait_send()
+    for i in range(1, STEPS):
+        for c in range(chunks):
+            sum_copy(i, 0, c, adj).wait_send()
+
+
+def on_line(tokens, router, expert_ids, gate_weight, up_weight, down_weight):
+    rows, width = tokens.shape
+    top = expert_ids.shape[1]
+    experts = router.shape[1]
+    hidden = gate_weight.shape[2]
+    cap = capacity_of(rows, top, experts)
+    chunks = 2
+    dma = pltpu.SemaphoreType.DMA
+    vmem = pl.BlockSpec(memory_space=pltpu.VMEM)
+    hbm = pl.BlockSpec(memory_space=pl.ANY)
+    flops = 6 * STEPS * 4 * cap * width * hidden
+    return pl.pallas_call(
+        functools.partial(moe_kernel, cap, chunks),
+        out_shape=jax.ShapeDtypeStruct((rows, width), BF16),
+        in_specs=[vmem, vmem, vmem, hbm, hbm, hbm],
+        out_specs=vmem,
+        scratch_shapes=[
+            pltpu.VMEM((width, hidden), BF16),
+            pltpu.VMEM((width, hidden), BF16),
+            pltpu.VMEM((hidden, width), BF16),
+            pltpu.VMEM((STEPS - 1, rows, width), BF16),
+            pltpu.VMEM((STEPS, experts, rows), F32),
+            pltpu.VMEM((STEPS, 4 * cap, width), BF16),
+            pltpu.VMEM((STEPS, cap, width), BF16),
+            pltpu.VMEM((2 * cap, width), F32),
+            pltpu.VMEM((STEPS, 2 * cap, width), BF16),
+            pltpu.VMEM((STEPS, 2 * cap, width), BF16),
+            pltpu.VMEM((STEPS, cap, width), BF16),
+            pltpu.VMEM((STEPS, 2 * cap, width), BF16),
+            pltpu.VMEM((STEPS, rows, width), F32),
+            pltpu.VMEM((STEPS - 1, rows, width), BF16),
+            pltpu.VMEM((5, rows, width), BF16),
+            dma((3,)),
+            dma((5,)),
+            dma((3,)),
+            dma((5,)),
+            dma((3,)),
+        ]
+        + [dma((STEPS,))] * 10
+        + [dma((3 * chunks,)), dma((5 * chunks,))],
+        compiler_params=pltpu.CompilerParams(
+            collective_id=0, has_side_effects=True, vmem_limit_bytes=56 * 2**20
+        ),
+        cost_estimate=pl.CostEstimate(
+            flops=flops, bytes_accessed=6 * width * hidden, transcendentals=0
+        ),
+    )(tokens, router, expert_ids, gate_weight, up_weight, down_weight)
+
+
+def capacity_of(rows, top, experts):
+    return min(rows, max(2, (5 * rows * top + 4 * experts - 1) // (4 * experts)))
 
 
 def slot_numbers(choices_flat, expert_count):
@@ -32,9 +414,7 @@
     tok_rows, model_width = tokens.shape
     top_count = expert_ids.shape[1]
     experts_all = router.shape[1]
-    capacity = min(
-        tok_rows, max(2, (5 * tok_rows * top_count + 4 * experts_all - 1) // (4 * experts_all))
-    )
+    capacity = capacity_of(tok_rows, top_count, experts_all)
     gate_share = router_gates(tokens, router, expert_ids)
     flat_ids = expert_ids.reshape(-1)
     target = flat_ids * capacity + slot_numbers(flat_ids, experts_all)
@@ -76,8 +456,9 @@
         P("exp", None, "tp"),
         P("exp", "tp", None),
     )
+    lined = mesh.shape["exp"] == 8 and mesh.shape["tp"] == 2
     return jax.shard_map(
-        on_device,
+        on_line if lined else on_device,
         mesh=mesh,
         in_specs=placed,
         out_specs=P(("grp", "exp", "tp"), None),

time: 262 us -> 120 us (0.46)
  Pallas kernels: 0 us -> 114 us
  blocking collectives: 89 us -> 0 us
  waiting for transfers between devices: 71.5 us -> 0 us
  matrix products: 31.1 us -> 0 us
  local copies, waits for them, and re-layouts: 29.1 us -> 5.15 us
  other arithmetic: 20.5 us -> 0 us
  between operations: 13.4 us -> 0.01 us
  starting transfers between devices: 5.91 us -> 0 us
    pallas_call x0 -> x1, Pallas kernels: none -> 114 us  [on_line(): pl.pallas_call(functools.partial(moe_kernel, cap, chunks), out_shape=jax....]
    all_to_all x2 -> x0, blocking collectives: 89 us -> none  [the longest x1 74.3 us: on_device(): lax.all_to_all(outgoing, 'exp', split_axis=0, concat_axis=0, tiled=True)]
    all_to_all x1 -> x0, waiting for transfers between devices: 56.7 us -> none  [on_device(): lax.all_to_all(own_share, 'exp', split_axis=0, concat_axis=0, tiled=True)]
    dot_general x4 -> x0, matrix products: 31.1 us -> none  [the longest x1 17.4 us: swiglu_part(): jnp.dot(hidden, down_part, preferred_element_type=jnp.float32)]
    all_gather x1 -> x0, waiting for transfers between devices: 14.7 us -> none  [on_device(): gathered = lax.all_gather(received, 'tp', axis=0, tiled=True)]
    reduce_sum x5 -> x0, other arithmetic: 14.2 us -> none  [the longest x1 6.54 us: on_device(): combined = jnp.sum(gate_share[:, :, None] * picked, axis=1)]
    gather x6 -> x0, local copies, waits for them, and re-layouts: 13.9 us -> none  [the longest x1 7.96 us: on_device(): flat_results[target].reshape(tok_rows, top_count, model_width)]
    all_to_all x1 -> x0, starting transfers between devices: 5.91 us -> none  [on_device(): lax.all_to_all(own_share, 'exp', split_axis=0, concat_axis=0, tiled=True)]
  transfers between devices with their start and end apart: 2 -> 0, of which waited for: 2 -> 0; matrix products, arithmetic and copies ran while one was open for 4% -> 0% of each run, Pallas kernels for 0% -> 0%
where the time goes in v1:
time: 120 us
  Pallas kernels  114 us (95%)
  local copies, waits for them, and re-layouts  5.15 us (4%)
    pallas_call x1, Pallas kernels, on_line(): pl.pallas_call(functools.partial(moe_kernel, cap, chunks), out_shape=jax....  114 us
    unnamed x3, local copies, waits for them, and re-layouts  5.15 us

profile of v1, /device:TPU:0, one launch (start us, length us, event | category | flops | bytes accessed | tf_op | source)
XLA Modules:
  0.0 119.6 jit_solution(8823107517897361694)
XLA Ops:
  0.0 1.4 %copy.8.ids_ref = s32[128,4]{1,0:T(8,128)} copy(s32[128,4]{0,1:T(4,128)} %param.8) | data formatting | bytes 4096 | tf_op args[2]
  1.4 1.8 %copy.7.router_ref = bf16[2304,8]{1,0:T(8,128)(2,1)} copy(bf16[2304,8]{0,1:T(8,128)(2,1)} %param.7) | data formatting | bytes 73728 | tf_op args[1]
  3.2 114.4 %shard_map.64 = bf16[128,2304]{1,0:T(8,128)(2,1)} custom-call(bf16[128,2304]{1,0:T(8,128)(2,1)} %tok_ref.1, bf16[2304,8]{1,0:T(8,128)(2,1)} %copy.7.router_ref, s32[128,4]{1,0:T(8,128)} %copy.8.ids_ref, bf16[1,2304,768]{2,1,0:T(8,128)(2,1)} %wg_hbm.1, bf16[1,2304,768]{2,1,0:T(8,128)(2,1)} %wu_hbm.1, bf16[1,768,2304]{2,1,0:T(8,128)(2,1)} %wd_hbm.1), custom_call_target="tpu_custom_call" | custom-call | flops 13589544960 | bytes 10616832 | tf_op jit(solution)/shard_map/pallas_call | solution.py:347
  117.6 1.9 %copy.10 = bf16[128,2304]{1,0:T(8,128)(2,1)} copy(bf16[128,2304]{1,0:T(8,128)(2,1)} %shard_map.64) | data formatting | bytes 1179648
